TPU v7x, 128 devices: a whole 4x4x4 slice. The times are simulated.
128 devices in a mesh: freq: 16 (over x_hi, y, core), stn: 8 (over x_lo, z).
Axes of the slice: x: 4 (x_hi: 2, x_lo: 2; x = x_hi * 2 + x_lo), y: 4, z: 4, core: 2. Of those that a mesh axis runs over, the one named last changes fastest.
Arguments:
- voltages: bfloat16 [1024, 32, 4096], P('stn', 'freq'), may hold values from -6 to 6
- filter_taps: float32 [16, 4096], replicated, may hold values from -1.5 to 1.5
- station_flags: int32 [512, 32], replicated, may hold values from 0 to 1, as said below
Outputs:
- visibilities: float32 [256, 1024, 1024], P('freq', 'stn')
Inputs may be any that keep to these rules, and one draw needn't show every extreme that they name: `station_flags`: 1 keeps a station's data in that spectrum, 0 flags it.
All inputs are finite; a program needn't handle non-finite values.
Results may differ from a plain program's by a relative error of at most 0.0039.
Values may be sent and summed in bfloat16 or wider, within the bound.
No kernel may reach another device: no remote copies, remote signals or barrier semaphores. Data moves between devices by JAX's collectives and lax.ppermute only.
A program may use at most 192 MiB of HBM per device.

v0:
```python
import math
import jax
import jax.numpy as jnp
from jax import lax
from jax.sharding import PartitionSpec as P

AVG = 16


def from_behind(block, axis, distance):
    devices = range(lax.axis_size(axis))
    route = [(i - distance, i) for i in devices if i - distance in devices]
    return lax.ppermute(block, axis, route)


def dct_four(rows):
    highest = lax.Precision.HIGHEST
    count_rows, channels = rows.shape
    inner_len = 128
    outer_len = channels // inner_len
    positions = jnp.arange(channels).astype(jnp.float32)
    theta = math.pi * positions / (2 * channels)
    real_part = (rows * jnp.cos(theta)).reshape(count_rows, outer_len, inner_len)
    imag_part = (-rows * jnp.sin(theta)).reshape(count_rows, outer_len, inner_len)
    outer_idx = jnp.arange(outer_len, dtype=jnp.int32)
    outer_phase = (
        2
        * math.pi
        * (outer_idx[:, None] * outer_idx[None, :] % outer_len).astype(jnp.float32)
        / outer_len
    )
    outer_cos = jnp.cos(outer_phase)
    outer_sin = jnp.sin(outer_phase)
    section_real = jnp.einsum("pab,ak->pkb", real_part, outer_cos, precision=highest) + jnp.einsum(
        "pab,ak->pkb", imag_part, outer_sin, precision=highest
    )
    section_imag = jnp.einsum("pab,ak->pkb", imag_part, outer_cos, precision=highest) - jnp.einsum(
        "pab,ak->pkb", real_part, outer_sin, precision=highest
    )
    inner_idx = jnp.arange(inner_len, dtype=jnp.int32)
    twist_phase = (
        2 * math.pi * (outer_idx[:, None] * inner_idx[None, :]).astype(jnp.float32) / channels
    )
    twist_cos = jnp.cos(twist_phase)
    twist_sin = jnp.sin(twist_phase)
    twist_real = section_real * twist_cos + section_imag * twist_sin
    twist_imag = section_imag * twist_cos - section_real * twist_sin
    inner_phase = (
        2
        * math.pi
        * (inner_idx[:, None] * inner_idx[None, :] % inner_len).astype(jnp.float32)
        / inner_len
    )
    inner_cos = jnp.cos(inner_phase)
    inner_sin = jnp.sin(inner_phase)
    final_real = jnp.einsum("pkb,bq->pqk", twist_real, inner_cos, precision=highest) + jnp.einsum(
        "pkb,bq->pqk", twist_imag, inner_sin, precision=highest
    )
    final_imag = jnp.einsum("pkb,bq->pqk", twist_imag, inner_cos, precision=highest) - jnp.einsum(
        "pkb,bq->pqk", twist_real, inner_sin, precision=highest
    )
    final_real = final_real.reshape(count_rows, channels)
    final_imag = final_imag.reshape(count_rows, channels)
    post_angle = math.pi * (2 * positions + 1) / (4 * channels)
    return math.sqrt(2.0 / channels) * (
        final_real * jnp.cos(post_angle) + final_imag * jnp.sin(post_angle)
    )


def make_tile(mine, theirs):
    return jnp.einsum("gax,gbx->gab", mine, theirs, preferred_element_type=jnp.float32)


def body(voltages, filter_taps, station_flags):
    sig_dev, spec_dev, channels = voltages.shape
    tap_count = filter_taps.shape[0]
    history_len = tap_count - 1
    reach_count = -(-history_len // spec_dev)
    earlier = []
    for distance in range(1, reach_count + 1):
        needed = min(spec_dev, history_len - (distance - 1) * spec_dev)
        earlier.append(from_behind(voltages[:, spec_dev - needed :, :], "freq", distance))
    frames = jnp.concatenate(earlier[::-1] + [voltages], axis=1)
    window = jnp.zeros((sig_dev, spec_dev, channels), jnp.float32)
    for tap_index in range(tap_count):
        offset = history_len - tap_index
        window = window + filter_taps[tap_index][None, None, :] * frames[
            :, offset : offset + spec_dev, :
        ].astype(jnp.float32)
    channelized = dct_four(window.reshape(sig_dev * spec_dev, channels)).astype(jnp.bfloat16)
    groups_all = channels // AVG
    arranged = (
        channelized.reshape(sig_dev, spec_dev, groups_all, AVG)
        .transpose(2, 0, 1, 3)
        .reshape(groups_all, sig_dev, spec_dev * AVG)
    )
    turned = lax.all_to_all(arranged, "freq", split_axis=0, concat_axis=2, tiled=True)
    signal_flags = jnp.repeat(station_flags, 2, axis=0).astype(jnp.float32)
    position = lax.axis_index("stn")
    own_flags = lax.dynamic_slice_in_dim(signal_flags, position * sig_dev, sig_dev, 0)
    keep = jnp.repeat(own_flags, AVG, axis=1).astype(jnp.bfloat16)
    local = turned * keep[None]
    counts = jnp.dot(own_flags, signal_flags.T, precision=lax.Precision.HIGHEST)
    denominator = AVG * jnp.maximum(counts, 1.0)
    totals = make_tile(local, lax.all_gather(local, "stn", axis=1, tiled=True))
    return totals / denominator[None]


def solution(mesh):
    in_specs = (P("stn", "freq", None), P(), P())
    out_specs = P("freq", "stn", None)
    return jax.shard_map(body, mesh=mesh, in_specs=in_specs, out_specs=out_specs, check_vma=False)
```

profile of v0, /device:TPU:1, one launch (start us, length us, event | category | flops | bytes accessed | tf_op | source)
XLA Modules:
  0.0 907.7 jit_solution(544670661215522051)
XLA Ops:
  6.5 4.7 collective-permute-start
  11.3 3.3 collective-permute-start.1
  14.6 4.1 slice.106
  19.8 4.6 collective-permute-start.7
  24.5 5.2 collective-permute-start.2
  32.3 14.6 %collective-permute-done.7 = bf16[128,1,4096]{2,0,1:T(8,128)(2,1)S(1)} collective-permute-done((bf16[128,1,4096]{2,0,1:T(8,128)(2,1)S(1)}, bf16[128,1,4096]{2,0,1:T(8,128)(2,1)S(1)}, u32[]{:S(2)}, u32[]{:S(2)}) %collective-permute-start.7) | collective-permute-done | bytes 1048608 | tf_op jit(solution)/shard_map/ppermute | solution.py:13
  46.9 62.1 %collective-permute-start.4 = (bf16[128,2,4096]{2,1,0:T(2,128)(2,1)S(1)}, bf16[128,2,4096]{2,1,0:T(2,128)(2,1)}, u32[]{:S(2)}, u32[]{:S(2)}) collective-permute-start(bf16[128,2,4096]{2,1,0:T(2,128)(2,1)S(1)} %copy-done.2), channel_id=1, source_target_pairs={{0,40},{8,48},{16,56},{24,64},{32,72},{40,80},{48,88},{56,96},{64,... | collective-permute-start | bytes 6291464 | tf_op jit(solution)/shard_map/ppermute | solution.py:13
  109.0 65.9 %collective-permute-start.5 = (bf16[128,2,4096]{2,1,0:T(2,128)(2,1)S(1)}, bf16[128,2,4096]{2,1,0:T(2,128)(2,1)}, u32[]{:S(2)}, u32[]{:S(2)}) collective-permute-start(bf16[128,2,4096]{2,1,0:T(2,128)(2,1)S(1)} %copy-done.2), channel_id=1, source_target_pairs={{0,48},{8,56},{16,64},{24,72},{32,80},{40,88},{48,96},{56,104},{64... | collective-permute-start | bytes 6291464 | tf_op jit(solution)/shard_map/ppermute | solution.py:13
  176.3 2.8 collective-permute-start.6
  184.7 4.5 collective-permute-done.3
  189.2 51.1 %collective-permute-done.5 = bf16[128,2,4096]{2,1,0:T(2,128)(2,1)} collective-permute-done((bf16[128,2,4096]{2,1,0:T(2,128)(2,1)S(1)}, bf16[128,2,4096]{2,1,0:T(2,128)(2,1)}, u32[]{:S(2)}, u32[]{:S(2)}) %collective-permute-start.5) | collective-permute-done | bytes 2097184 | tf_op jit(solution)/shard_map/ppermute | solution.py:13
  240.3 61.7 %multiply_add_fusion = f32[128,2,4096]{2,1,0:T(2,128)} fusion(bf16[128,2,4096]{2,1,0:T(2,128)(2,1)} %collective-permute-done.6, bf16[128,2,4096]{2,1,0:T(2,128)(2,1)} %collective-permute-done.5, bf16[128,2,4096]{2,1,0:T(2,128)(2,1)} %collective-permute-done.4, bf16[128,2,4096]{2,1,0:T(2,128)(2,1)} %collective-permute-done.3, ...), kind=kLoop, calls=%fused_computation.8 | loop fusion | flops 74448896 | bytes 22282240 | tf_op jit(solution)/shard_map/add | solution.py:87
  302.0 6.6 reshape.108
  308.6 6.0 fusion.14
  314.6 4.1 fusion.9
  318.7 4.4 fusion.20
  323.1 5.1 add_bitcast_fusion.1
  328.3 6.0 fusion.3
  334.3 8.3 fusion.1
  342.5 8.0 add_bitcast_fusion
  350.5 14.5 %copy.49 = f32[256,128,32]{2,1,0:T(8,128)} copy(f32[256,128,32]{0,1,2:T(8,128)} %add_bitcast_fusion) | data formatting | bytes 8388608 | tf_op jit(solution)/shard_map/add | solution.py:56
  365.0 24.6 %reshape.109 = f32[128,2,256,16]{3,2,1,0:T(8,128)} reshape(f32[256,128,32]{2,1,0:T(8,128)} %copy.49) | data formatting | bytes 8388608 | tf_op jit(solution)/shard_map/reshape | solution.py:62
  389.7 11.4 %subtract_bitcast_fusion = f32[256,128,32]{0,1,2:T(8,128)} fusion(f32[128,256,32]{1,0,2:T(8,128)} %fusion.1, f32[256,32,128]{2,1,0:T(8,128)} %copy-done.1), kind=kOutput, calls=%fused_computation.3 | convolution fusion | flops 1611890688 | bytes 12582912 | tf_op jit(solution)/shard_map/pkb,bq->pqk/dot_general | solution.py:59
  401.1 14.5 %copy.53 = f32[256,128,32]{2,1,0:T(8,128)} copy(f32[256,128,32]{0,1,2:T(8,128)} %subtract_bitcast_fusion) | data formatting | bytes 8388608 | tf_op jit(solution)/shard_map/sub | solution.py:59
  415.7 24.4 %reshape.110 = f32[128,2,256,16]{3,2,1,0:T(8,128)} reshape(f32[256,128,32]{2,1,0:T(8,128)} %copy.53) | data formatting | bytes 8388608 | tf_op jit(solution)/shard_map/reshape | solution.py:63
  440.1 27.8 %fusion = bf16[256,128,2,16]{3,0,2,1:T(8,128)(2,1)} fusion(f32[128,2,256,16]{3,2,1,0:T(8,128)} %reshape.110, f32[128,2,256,16]{3,2,1,0:T(8,128)} %reshape.109, f32[256,16]{1,0:T(8,128)S(1)} %copy.54, f32[256,16]{1,0:T(8,128)S(1)} %copy.50), kind=kLoop, calls=%fused_computation.1 | loop fusion | flops 5242880 | bytes 10518528 | tf_op jit(solution)/shard_map/transpose | solution.py:94
  467.8 15.4 %copy.55 = bf16[256,128,2,16]{1,3,2,0:T(8,128)(2,1)} copy(bf16[256,128,2,16]{3,0,2,1:T(8,128)(2,1)} %fusion) | data formatting | bytes 4194304 | tf_op jit(solution)/shard_map/transpose | solution.py:94
  483.2 197.7 %all-to-all-start = ((bf16[256,128,32]{1,2,0:T(8,128)(2,1)}), bf16[256,128,32]{1,2,0:T(8,128)(2,1)S(1)}, u32[]{:S(2)}, u32[]{:S(2)}) async-start(bf16[256,128,32]{1,2,0:T(8,128)(2,1)} %bitcast.25), calls=%async_computation | async-start | bytes 4194304 | tf_op jit(solution)/shard_map/all_to_all | solution.py:97
  681.6 27.8 %all-to-all-done = bf16[256,128,32]{1,2,0:T(8,128)(2,1)S(1)} async-done(((bf16[256,128,32]{1,2,0:T(8,128)(2,1)}), bf16[256,128,32]{1,2,0:T(8,128)(2,1)S(1)}, u32[]{:S(2)}, u32[]{:S(2)}) %all-to-all-start) | async-done | bytes 2097184 | tf_op jit(solution)/shard_map/all_to_all | solution.py:97
  711.3 3.1 copy.60
  716.5 172.2 %all-gather.2.cloned.1.call-done = bf16[16,1024,512]{2,1,0:T(8,128)(2,1)} async-done(((bf16[16,128,512]{2,1,0:T(8,128)(2,1)}), bf16[16,1024,512]{2,1,0:T(8,128)(2,1)}) %all-gather.2.cloned.1.call-update) | async-done | bytes 16777232 | tf_op jit(solution)/shard_map/all_gather | solution.py:105
  888.7 11.7 %broadcast_divide_fusion = f32[16,128,1024]{2,1,0:T(8,128)} fusion(f32[128,1024]{1,0:T(8,128)S(1)} %fusion.27, bf16[16,128,512]{2,1,0:T(8,128)(2,1)} %broadcast_multiply_fusion, bf16[16,1024,512]{2,1,0:T(8,128)(2,1)} %all-gather.2.cloned.1.call-done), kind=kOutput, calls=%fused_computation.2 | convolution fusion | flops 2149580800 | bytes 27787264 | tf_op jit(solution)/shard_map/gax,gbx->gab/dot_general | solution.py:71
  (42 shorter events, 15.2 us)
Async XLA Ops:
  6.5 17.9 %copy-start.2 = (bf16[128,2,4096]{2,1,0:T(2,128)(2,1)S(1)}, bf16[128,2,4096]{2,1,0:T(2,128)(2,1)}, u32[]{:S(2)}) copy-start(bf16[128,2,4096]{2,1,0:T(2,128)(2,1)} %param.3) | copy-start | bytes 6291460
  6.5 102.5 %collective-permute-start = (bf16[128,2,4096]{2,1,0:T(2,128)(2,1)}, bf16[128,2,4096]{2,1,0:T(2,128)(2,1)S(1)}, u32[]{:S(2)}, u32[]{:S(2)}) collective-permute-start(bf16[128,2,4096]{2,1,0:T(2,128)(2,1)} %param.3), channel_id=1, source_target_pairs={{0,8},{8,16},{16,24},{24,32},{32,40},{40,48},{48,56},{56,64},{64,7... | collective-permute-start | bytes 6291464 | tf_op jit(solution)/shard_map/ppermute | solution.py:13
  11.3 163.7 %collective-permute-start.1 = (bf16[128,2,4096]{2,1,0:T(2,128)(2,1)}, bf16[128,2,4096]{2,1,0:T(2,128)(2,1)S(1)}, u32[]{:S(2)}, u32[]{:S(2)}) collective-permute-start(bf16[128,2,4096]{2,1,0:T(2,128)(2,1)} %param.3), channel_id=1, source_target_pairs={{0,16},{8,24},{16,32},{24,40},{32,48},{40,56},{48,64},{56,72},{64,... | collective-permute-start | bytes 6291464 | tf_op jit(solution)/shard_map/ppermute | solution.py:13
  19.8 27.1 %collective-permute-start.7 = (bf16[128,1,4096]{2,0,1:T(8,128)(2,1)S(1)}, bf16[128,1,4096]{2,0,1:T(8,128)(2,1)S(1)}, u32[]{:S(2)}, u32[]{:S(2)}) collective-permute-start(bf16[128,1,4096]{2,0,1:T(8,128)(2,1)S(1)} %copy.61), channel_id=1, source_target_pairs={{0,64},{8,72},{16,80},{24,88},{32,96},{40,104},{48,112},{56,120},{... | collective-permute-start | bytes 3145736 | tf_op jit(solution)/shard_map/ppermute | solution.py:13
  24.5 160.2 %collective-permute-start.2 = (bf16[128,2,4096]{2,1,0:T(2,128)(2,1)S(1)}, bf16[128,2,4096]{2,1,0:T(2,128)(2,1)}, u32[]{:S(2)}, u32[]{:S(2)}) collective-permute-start(bf16[128,2,4096]{2,1,0:T(2,128)(2,1)S(1)} %copy-done.2), channel_id=1, source_target_pairs={{0,24},{8,32},{16,40},{24,48},{32,56},{40,64},{48,72},{56,80},{64,... | collective-permute-start | bytes 6291464 | tf_op jit(solution)/shard_map/ppermute | solution.py:13
  29.7 159.5 %collective-permute-start.3 = (bf16[128,2,4096]{2,1,0:T(2,128)(2,1)S(1)}, bf16[128,2,4096]{2,1,0:T(2,128)(2,1)}, u32[]{:S(2)}, u32[]{:S(2)}) collective-permute-start(bf16[128,2,4096]{2,1,0:T(2,128)(2,1)S(1)} %copy-done.2), channel_id=1, source_target_pairs={{0,32},{8,40},{16,48},{24,56},{32,64},{40,72},{48,80},{56,88},{64,... | collective-permute-start | bytes 6291464 | tf_op jit(solution)/shard_map/ppermute | solution.py:13
  46.9 142.3 %collective-permute-start.4 = (bf16[128,2,4096]{2,1,0:T(2,128)(2,1)S(1)}, bf16[128,2,4096]{2,1,0:T(2,128)(2,1)}, u32[]{:S(2)}, u32[]{:S(2)}) collective-permute-start(bf16[128,2,4096]{2,1,0:T(2,128)(2,1)S(1)} %copy-done.2), channel_id=1, source_target_pairs={{0,40},{8,48},{16,56},{24,64},{32,72},{40,80},{48,88},{56,96},{64,... | collective-permute-start | bytes 6291464 | tf_op jit(solution)/shard_map/ppermute | solution.py:13
  109.0 65.9 %copy-start.3 = (bf16[128,2,4096]{2,1,0:T(2,128)(2,1)}, bf16[128,2,4096]{2,1,0:T(2,128)(2,1)S(1)}, u32[]{:S(2)}) copy-start(bf16[128,2,4096]{2,1,0:T(2,128)(2,1)S(1)} %collective-permute-done) | copy-start | bytes 6291460
  109.0 131.3 %collective-permute-start.5 = (bf16[128,2,4096]{2,1,0:T(2,128)(2,1)S(1)}, bf16[128,2,4096]{2,1,0:T(2,128)(2,1)}, u32[]{:S(2)}, u32[]{:S(2)}) collective-permute-start(bf16[128,2,4096]{2,1,0:T(2,128)(2,1)S(1)} %copy-done.2), channel_id=1, source_target_pairs={{0,48},{8,56},{16,64},{24,72},{32,80},{40,88},{48,96},{56,104},{64... | collective-permute-start | bytes 6291464 | tf_op jit(solution)/shard_map/ppermute | solution.py:13
  174.9 1.3 copy-start.5
  176.3 64.1 %collective-permute-start.6 = (bf16[128,2,4096]{2,1,0:T(2,128)(2,1)S(1)}, bf16[128,2,4096]{2,1,0:T(2,128)(2,1)}, u32[]{:S(2)}, u32[]{:S(2)}) collective-permute-start(bf16[128,2,4096]{2,1,0:T(2,128)(2,1)S(1)} %copy-done.2), channel_id=1, source_target_pairs={{0,56},{8,64},{16,72},{24,80},{32,88},{40,96},{48,104},{56,112},{6... | collective-permute-start | bytes 6291464 | tf_op jit(solution)/shard_map/ppermute | solution.py:13
  179.4 60.9 %copy-start.4 = (bf16[128,2,4096]{2,1,0:T(2,128)(2,1)S(1)}, bf16[128,2,4096]{2,1,0:T(2,128)(2,1)}, u32[]{:S(2)}) copy-start(bf16[128,2,4096]{2,1,0:T(2,128)(2,1)} %copy-done.3) | copy-start | bytes 6291460
  308.6 6.0 copy-start
  328.2 14.3 %copy-start.1 = (f32[256,32,128]{2,1,0:T(8,128)}, f32[256,32,128]{2,1,0:T(8,128)S(1)}, u32[]{:S(2)}) copy-start(f32[256,32,128]{2,1,0:T(8,128)S(1)} %get-tuple-element.5) | copy-start | bytes 12582916
  483.2 197.7 %copy-start.6 = (s32[512,32]{0,1:T(8,128)S(1)}, s32[512,32]{0,1:T(8,128)}, u32[]{:S(2)}) copy-start(s32[512,32]{0,1:T(8,128)} %param.5) | copy-start | bytes 196612
  483.2 226.2 %all-to-all-start = ((bf16[256,128,32]{1,2,0:T(8,128)(2,1)}), bf16[256,128,32]{1,2,0:T(8,128)(2,1)S(1)}, u32[]{:S(2)}, u32[]{:S(2)}) async-start(bf16[256,128,32]{1,2,0:T(8,128)(2,1)} %bitcast.25), calls=%async_computation | async-start | bytes 4194304 | tf_op jit(solution)/shard_map/all_to_all | solution.py:97
  680.9 207.8 %all-gather.2.cloned.1.call-start = ((), (), s32[]{:S(2)}) async-start(), calls=%async_computation.1 | async-start | bytes 18874368 | tf_op jit(solution)/shard_map/all_gather | solution.py:105
Sparse Core Ops, SparseCore 0:
  716.0 172.6 all-gather.1
where the time goes:
time: 914 us; the launch traced here: 908 us
  starting transfers between devices  349 us (38%)
  waiting for transfers between devices  270 us (30%)
  local copies, waits for them, and re-layouts  117 us (13%)
  other arithmetic  91.3 us (10%)
  matrix products  65.6 us (7%)
  between operations  14.2 us (2%)
    all_to_all x1, starting transfers between devices, body(): lax.all_to_all(arranged, 'freq', split_axis=0, concat_axis=2, tiled=True)  198 us
    all_gather x1, waiting for transfers between devices, body(): totals = make_tile(local, lax.all_gather(local, 'stn', axis=1, tiled=True))  172 us
    ppermute x8, starting transfers between devices, from_behind(): return lax.ppermute(block, axis, route)  151 us
    ppermute x8, waiting for transfers between devices, from_behind(): return lax.ppermute(block, axis, route)  70.3 us
    add x1, other arithmetic, body(): window + filter_taps[tap_index][None, None, :] * frames[:, offset:offset...  61.7 us
    all_to_all x1, waiting for transfers between devices, body(): lax.all_to_all(arranged, 'freq', split_axis=0, concat_axis=2, tiled=True)  27.8 us
    transpose x1, other arithmetic, body(): arranged = channelized.reshape(sig_dev, spec_dev, groups_all, AVG).transp...  27.8 us
    reshape x1, local copies, waits for them, and re-layouts, dct_four(): final_real = final_real.reshape(count_rows, channels)  24.6 us
  transfers between devices with their start and end apart: 10, of which 5 were waited for; matrix products, arithmetic and copies ran while one was open for 1% of the time, Pallas kernels for 0%

commit v1 on v0

--- a/solution.py
+++ b/solution.py
@@ -94,7 +94,10 @@
         .transpose(2, 0, 1, 3)
         .reshape(groups_all, sig_dev, spec_dev * AVG)
     )
-    turned = lax.all_to_all(arranged, "freq", split_axis=0, concat_axis=2, tiled=True)
+    turned = jnp.concatenate(
+        lax.all_to_all(jnp.stack(jnp.split(arranged, lax.axis_size("freq"), axis=0)), "freq", 0, 0),
+        axis=2,
+    )
     signal_flags = jnp.repeat(station_flags, 2, axis=0).astype(jnp.float32)
     position = lax.axis_index("stn")
     own_flags = lax.dynamic_slice_in_dim(signal_flags, position * sig_dev, sig_dev, 0)

time: 914 us -> 965 us (1.056)
  local copies, waits for them, and re-layouts: 117 us -> 168 us
    split x0 -> x17, local copies, waits for them, and re-layouts: none -> 49.6 us  [body(): jnp.split(arranged, lax.axis_size('freq'), axis=0)]
    unnamed x17 -> x38, local copies, waits for them, and re-layouts: 2.57 us -> 18.9 us
    transpose x1 -> x0, local copies, waits for them, and re-layouts: 15.4 us -> none  [body(): arranged = channelized.reshape(sig_dev, spec_dev, groups_all, AVG).transp...]
where the time goes in v1:
time: 965 us; the launch traced here: 958 us
  starting transfers between devices  349 us (36%)
  waiting for transfers between devices  270 us (28%)
  local copies, waits for them, and re-layouts  168 us (17%)
  other arithmetic  91.2 us (9%)
  matrix products  65.5 us (7%)
  between operations  14 us (1%)
    all_to_all x1, starting transfers between devices, body(): lax.all_to_all(jnp.stack(jnp.split(arranged, lax.axis_size('freq'), axis=...  198 us
    all_gather x1, waiting for transfers between devices, body(): totals = make_tile(local, lax.all_gather(local, 'stn', axis=1, tiled=True))  172 us
    ppermute x8, starting transfers between devices, from_behind(): return lax.ppermute(block, axis, route)  152 us
    ppermute x8, waiting for transfers between devices, from_behind(): return lax.ppermute(block, axis, route)  70.1 us
    add x1, other arithmetic, body(): window + filter_taps[tap_index][None, None, :] * frames[:, offset:offset...  61.6 us
    split x17, local copies, waits for them, and re-layouts, body(): jnp.split(arranged, lax.axis_size('freq'), axis=0)  49.6 us
    all_to_all x1, waiting for transfers between devices, body(): lax.all_to_all(jnp.stack(jnp.split(arranged, lax.axis_size('freq'), axis=...  27.8 us
    transpose x1, other arithmetic, body(): arranged = channelized.reshape(sig_dev, spec_dev, groups_all, AVG).transp...  27.7 us
  transfers between devices with their start and end apart: 10, of which 5 were waited for; matrix products, arithmetic and copies ran while one was open for 1% of the time, Pallas kernels for 0%

profile of v1, /device:TPU:1, one launch (start us, length us, event | category | flops | bytes accessed | tf_op | source)
XLA Modules:
  0.0 958.1 jit_solution(7138966283315117398)
XLA Ops:
  6.5 4.7 collective-permute-start
  11.3 3.3 collective-permute-start.1
  14.6 4.1 slice.122
  19.8 4.6 collective-permute-start.7
  24.5 5.2 collective-permute-start.2
  32.4 14.6 %collective-permute-done.7 = bf16[128,1,4096]{2,0,1:T(8,128)(2,1)S(1)} collective-permute-done((bf16[128,1,4096]{2,0,1:T(8,128)(2,1)S(1)}, bf16[128,1,4096]{2,0,1:T(8,128)(2,1)S(1)}, u32[]{:S(2)}, u32[]{:S(2)}) %collective-permute-start.7) | collective-permute-done | bytes 1048608 | tf_op jit(solution)/shard_map/ppermute | solution.py:13
  46.9 62.1 %collective-permute-start.4 = (bf16[128,2,4096]{2,1,0:T(2,128)(2,1)S(1)}, bf16[128,2,4096]{2,1,0:T(2,128)(2,1)}, u32[]{:S(2)}, u32[]{:S(2)}) collective-permute-start(bf16[128,2,4096]{2,1,0:T(2,128)(2,1)S(1)} %copy-done.2), channel_id=1, source_target_pairs={{0,40},{8,48},{16,56},{24,64},{32,72},{40,80},{48,88},{56,96},{64,... | collective-permute-start | bytes 6291464 | tf_op jit(solution)/shard_map/ppermute | solution.py:13
  109.0 65.9 %collective-permute-start.5 = (bf16[128,2,4096]{2,1,0:T(2,128)(2,1)S(1)}, bf16[128,2,4096]{2,1,0:T(2,128)(2,1)}, u32[]{:S(2)}, u32[]{:S(2)}) collective-permute-start(bf16[128,2,4096]{2,1,0:T(2,128)(2,1)S(1)} %copy-done.2), channel_id=1, source_target_pairs={{0,48},{8,56},{16,64},{24,72},{32,80},{40,88},{48,96},{56,104},{64... | collective-permute-start | bytes 6291464 | tf_op jit(solution)/shard_map/ppermute | solution.py:13
  176.3 3.1 collective-permute-start.6
  184.8 4.4 collective-permute-done.3
  189.2 51.1 %collective-permute-done.5 = bf16[128,2,4096]{2,1,0:T(2,128)(2,1)} collective-permute-done((bf16[128,2,4096]{2,1,0:T(2,128)(2,1)S(1)}, bf16[128,2,4096]{2,1,0:T(2,128)(2,1)}, u32[]{:S(2)}, u32[]{:S(2)}) %collective-permute-start.5) | collective-permute-done | bytes 2097184 | tf_op jit(solution)/shard_map/ppermute | solution.py:13
  240.3 61.6 %multiply_add_fusion = f32[128,2,4096]{2,1,0:T(2,128)} fusion(bf16[128,2,4096]{2,1,0:T(2,128)(2,1)} %collective-permute-done.6, bf16[128,2,4096]{2,1,0:T(2,128)(2,1)} %collective-permute-done.5, bf16[128,2,4096]{2,1,0:T(2,128)(2,1)} %collective-permute-done.4, bf16[128,2,4096]{2,1,0:T(2,128)(2,1)} %collective-permute-done.3, ...), kind=kLoop, calls=%fused_computation.8 | loop fusion | flops 74448896 | bytes 22282240 | tf_op jit(solution)/shard_map/add | solution.py:87
  301.9 6.6 reshape.144
  308.5 5.7 fusion.14
  314.3 4.1 fusion.9
  318.3 4.4 fusion.20
  322.8 5.1 add_bitcast_fusion.1
  327.9 6.0 fusion.3
  333.9 8.5 fusion.1
  342.4 8.0 add_bitcast_fusion
  350.3 14.5 %copy.94 = f32[256,128,32]{2,1,0:T(8,128)} copy(f32[256,128,32]{0,1,2:T(8,128)} %add_bitcast_fusion) | data formatting | bytes 8388608 | tf_op jit(solution)/shard_map/add | solution.py:56
  364.9 24.6 %reshape.145 = f32[128,2,256,16]{3,2,1,0:T(8,128)} reshape(f32[256,128,32]{2,1,0:T(8,128)} %copy.94) | data formatting | bytes 8388608 | tf_op jit(solution)/shard_map/reshape | solution.py:62
  389.5 11.4 %subtract_bitcast_fusion = f32[256,128,32]{0,1,2:T(8,128)} fusion(f32[128,256,32]{1,0,2:T(8,128)} %fusion.1, f32[256,32,128]{2,1,0:T(8,128)} %copy-done.1), kind=kOutput, calls=%fused_computation.3 | convolution fusion | flops 1611890688 | bytes 12582912 | tf_op jit(solution)/shard_map/pkb,bq->pqk/dot_general | solution.py:59
  400.9 14.5 %copy.98 = f32[256,128,32]{2,1,0:T(8,128)} copy(f32[256,128,32]{0,1,2:T(8,128)} %subtract_bitcast_fusion) | data formatting | bytes 8388608 | tf_op jit(solution)/shard_map/sub | solution.py:59
  415.4 24.4 %reshape.146 = f32[128,2,256,16]{3,2,1,0:T(8,128)} reshape(f32[256,128,32]{2,1,0:T(8,128)} %copy.98) | data formatting | bytes 8388608 | tf_op jit(solution)/shard_map/reshape | solution.py:63
  439.9 27.7 %fusion = bf16[256,128,2,16]{3,0,2,1:T(8,128)(2,1)} fusion(f32[128,2,256,16]{3,2,1,0:T(8,128)} %reshape.146, f32[128,2,256,16]{3,2,1,0:T(8,128)} %reshape.145, f32[256,16]{1,0:T(8,128)S(1)} %copy.99, f32[256,16]{1,0:T(8,128)S(1)} %copy.95), kind=kLoop, calls=%fused_computation.1 | loop fusion | flops 5242880 | bytes 10518528 | tf_op jit(solution)/shard_map/transpose | solution.py:94
  467.6 11.7 %fusion.98 = (bf16[16,128,2,16]{3,0,2,1:T(8,128)(2,1)S(1)}, bf16[16,128,2,16]{3,0,2,1:T(8,128)(2,1)S(1)}, bf16[16,128,2,16]{3,0,2,1:T(8,128)(2,1)S(1)}, bf16[16,...) fusion(bf16[256,128,2,16]{3,0,2,1:T(8,128)(2,1)} %fusion), kind=kLoop, calls=%fused_computation.128 | loop fusion | bytes 4194304 | tf_op jit(solution)/shard_map/split | solution.py:98
  534.2 197.6 %all-to-all-start = ((bf16[16,16,128,32]{2,3,1,0:T(8,128)(2,1)}), bf16[16,16,128,32]{2,3,1,0:T(8,128)(2,1)S(1)}, u32[]{:S(2)}, u32[]{:S(2)}) async-start(bf16[16,16,128,32]{2,3,1,0:T(8,128)(2,1)} %constant_dynamic-update-slice_fusion), calls=%async_computation | async-start | bytes 4194304 | tf_op jit(solution)/shard_map/all_to_all | solution.py:98
  732.5 27.8 %all-to-all-done = bf16[16,16,128,32]{2,3,1,0:T(8,128)(2,1)S(1)} async-done(((bf16[16,16,128,32]{2,3,1,0:T(8,128)(2,1)}), bf16[16,16,128,32]{2,3,1,0:T(8,128)(2,1)S(1)}, u32[]{:S(2)}, u32[]{:S(2)}) %all-to-all-start) | async-done | bytes 2097184 | tf_op jit(solution)/shard_map/all_to_all | solution.py:98
  762.2 2.9 copy.120
  767.1 172.2 %all-gather.2.cloned.1.call-done = bf16[16,1024,512]{2,1,0:T(8,128)(2,1)} async-done(((bf16[16,128,512]{2,1,0:T(8,128)(2,1)}), bf16[16,1024,512]{2,1,0:T(8,128)(2,1)}) %all-gather.2.cloned.1.call-update) | async-done | bytes 16777232 | tf_op jit(solution)/shard_map/all_gather | solution.py:108
  939.3 11.7 %broadcast_divide_fusion = f32[16,128,1024]{2,1,0:T(8,128)} fusion(f32[128,1024]{1,0:T(8,128)S(1)} %fusion.27, bf16[16,128,512]{2,1,0:T(8,128)(2,1)} %broadcast_multiply_fusion, bf16[16,1024,512]{2,1,0:T(8,128)(2,1)} %all-gather.2.cloned.1.call-done), kind=kOutput, calls=%fused_computation.2 | convolution fusion | flops 2149580800 | bytes 27787264 | tf_op jit(solution)/shard_map/gax,gbx->gab/dot_general | solution.py:71
  (80 shorter events, 70.0 us)
Async XLA Ops:
  6.5 17.9 %copy-start.2 = (bf16[128,2,4096]{2,1,0:T(2,128)(2,1)S(1)}, bf16[128,2,4096]{2,1,0:T(2,128)(2,1)}, u32[]{:S(2)}) copy-start(bf16[128,2,4096]{2,1,0:T(2,128)(2,1)} %param.3) | copy-start | bytes 6291460
  6.5 102.5 %collective-permute-start = (bf16[128,2,4096]{2,1,0:T(2,128)(2,1)}, bf16[128,2,4096]{2,1,0:T(2,128)(2,1)S(1)}, u32[]{:S(2)}, u32[]{:S(2)}) collective-permute-start(bf16[128,2,4096]{2,1,0:T(2,128)(2,1)} %param.3), channel_id=1, source_target_pairs={{0,8},{8,16},{16,24},{24,32},{32,40},{40,48},{48,56},{56,64},{64,7... | collective-permute-start | bytes 6291464 | tf_op jit(solution)/shard_map/ppermute | solution.py:13
  11.3 163.7 %collective-permute-start.1 = (bf16[128,2,4096]{2,1,0:T(2,128)(2,1)}, bf16[128,2,4096]{2,1,0:T(2,128)(2,1)S(1)}, u32[]{:S(2)}, u32[]{:S(2)}) collective-permute-start(bf16[128,2,4096]{2,1,0:T(2,128)(2,1)} %param.3), channel_id=1, source_target_pairs={{0,16},{8,24},{16,32},{24,40},{32,48},{40,56},{48,64},{56,72},{64,... | collective-permute-start | bytes 6291464 | tf_op jit(solution)/shard_map/ppermute | solution.py:13
  19.8 27.1 %collective-permute-start.7 = (bf16[128,1,4096]{2,0,1:T(8,128)(2,1)S(1)}, bf16[128,1,4096]{2,0,1:T(8,128)(2,1)S(1)}, u32[]{:S(2)}, u32[]{:S(2)}) collective-permute-start(bf16[128,1,4096]{2,0,1:T(8,128)(2,1)S(1)} %copy.121), channel_id=1, source_target_pairs={{0,64},{8,72},{16,80},{24,88},{32,96},{40,104},{48,112},{56,120},{... | collective-permute-start | bytes 3145736 | tf_op jit(solution)/shard_map/ppermute | solution.py:13
  24.5 160.3 %collective-permute-start.2 = (bf16[128,2,4096]{2,1,0:T(2,128)(2,1)S(1)}, bf16[128,2,4096]{2,1,0:T(2,128)(2,1)}, u32[]{:S(2)}, u32[]{:S(2)}) collective-permute-start(bf16[128,2,4096]{2,1,0:T(2,128)(2,1)S(1)} %copy-done.2), channel_id=1, source_target_pairs={{0,24},{8,32},{16,40},{24,48},{32,56},{40,64},{48,72},{56,80},{64,... | collective-permute-start | bytes 6291464 | tf_op jit(solution)/shard_map/ppermute | solution.py:13
  29.7 159.5 %collective-permute-start.3 = (bf16[128,2,4096]{2,1,0:T(2,128)(2,1)S(1)}, bf16[128,2,4096]{2,1,0:T(2,128)(2,1)}, u32[]{:S(2)}, u32[]{:S(2)}) collective-permute-start(bf16[128,2,4096]{2,1,0:T(2,128)(2,1)S(1)} %copy-done.2), channel_id=1, source_target_pairs={{0,32},{8,40},{16,48},{24,56},{32,64},{40,72},{48,80},{56,88},{64,... | collective-permute-start | bytes 6291464 | tf_op jit(solution)/shard_map/ppermute | solution.py:13
  46.9 142.3 %collective-permute-start.4 = (bf16[128,2,4096]{2,1,0:T(2,128)(2,1)S(1)}, bf16[128,2,4096]{2,1,0:T(2,128)(2,1)}, u32[]{:S(2)}, u32[]{:S(2)}) collective-permute-start(bf16[128,2,4096]{2,1,0:T(2,128)(2,1)S(1)} %copy-done.2), channel_id=1, source_target_pairs={{0,40},{8,48},{16,56},{24,64},{32,72},{40,80},{48,88},{56,96},{64,... | collective-permute-start | bytes 6291464 | tf_op jit(solution)/shard_map/ppermute | solution.py:13
  109.0 65.9 %copy-start.3 = (bf16[128,2,4096]{2,1,0:T(2,128)(2,1)}, bf16[128,2,4096]{2,1,0:T(2,128)(2,1)S(1)}, u32[]{:S(2)}) copy-start(bf16[128,2,4096]{2,1,0:T(2,128)(2,1)S(1)} %collective-permute-done) | copy-start | bytes 6291460
  109.0 131.3 %collective-permute-start.5 = (bf16[128,2,4096]{2,1,0:T(2,128)(2,1)S(1)}, bf16[128,2,4096]{2,1,0:T(2,128)(2,1)}, u32[]{:S(2)}, u32[]{:S(2)}) collective-permute-start(bf16[128,2,4096]{2,1,0:T(2,128)(2,1)S(1)} %copy-done.2), channel_id=1, source_target_pairs={{0,48},{8,56},{16,64},{24,72},{32,80},{40,88},{48,96},{56,104},{64... | collective-permute-start | bytes 6291464 | tf_op jit(solution)/shard_map/ppermute | solution.py:13
  174.9 1.3 copy-start.5
  176.3 64.1 %collective-permute-start.6 = (bf16[128,2,4096]{2,1,0:T(2,128)(2,1)S(1)}, bf16[128,2,4096]{2,1,0:T(2,128)(2,1)}, u32[]{:S(2)}, u32[]{:S(2)}) collective-permute-start(bf16[128,2,4096]{2,1,0:T(2,128)(2,1)S(1)} %copy-done.2), channel_id=1, source_target_pairs={{0,56},{8,64},{16,72},{24,80},{32,88},{40,96},{48,104},{56,112},{6... | collective-permute-start | bytes 6291464 | tf_op jit(solution)/shard_map/ppermute | solution.py:13
  179.8 60.6 %copy-start.4 = (bf16[128,2,4096]{2,1,0:T(2,128)(2,1)S(1)}, bf16[128,2,4096]{2,1,0:T(2,128)(2,1)}, u32[]{:S(2)}) copy-start(bf16[128,2,4096]{2,1,0:T(2,128)(2,1)} %copy-done.3) | copy-start | bytes 6291460
  308.5 5.8 copy-start
  327.9 14.5 %copy-start.1 = (f32[256,32,128]{2,1,0:T(8,128)}, f32[256,32,128]{2,1,0:T(8,128)S(1)}, u32[]{:S(2)}) copy-start(f32[256,32,128]{2,1,0:T(8,128)S(1)} %get-tuple-element.21) | copy-start | bytes 12582916
  515.8 13.1 %copy-start.8 = (bf16[16,128,2,16]{1,3,2,0:T(8,128)(2,1)S(1)}, bf16[16,128,2,16]{1,3,2,0:T(8,128)(2,1)}, u32[]{:S(2)}) copy-start(bf16[16,128,2,16]{1,3,2,0:T(8,128)(2,1)} %copy.108) | copy-start | bytes 393220
  515.8 13.8 %copy-start.7 = (bf16[16,128,2,16]{1,3,2,0:T(8,128)(2,1)S(1)}, bf16[16,128,2,16]{1,3,2,0:T(8,128)(2,1)}, u32[]{:S(2)}) copy-start(bf16[16,128,2,16]{1,3,2,0:T(8,128)(2,1)} %copy.109) | copy-start | bytes 393220
  515.8 14.4 %copy-start.6 = (bf16[16,128,2,16]{1,3,2,0:T(8,128)(2,1)S(1)}, bf16[16,128,2,16]{1,3,2,0:T(8,128)(2,1)}, u32[]{:S(2)}) copy-start(bf16[16,128,2,16]{1,3,2,0:T(8,128)(2,1)} %copy.110) | copy-start | bytes 393220
  517.9 213.9 %copy-start.9 = (s32[512,32]{0,1:T(8,128)S(1)}, s32[512,32]{0,1:T(8,128)}, u32[]{:S(2)}) copy-start(s32[512,32]{0,1:T(8,128)} %param.5) | copy-start | bytes 196612
  534.2 226.0 %all-to-all-start = ((bf16[16,16,128,32]{2,3,1,0:T(8,128)(2,1)}), bf16[16,16,128,32]{2,3,1,0:T(8,128)(2,1)S(1)}, u32[]{:S(2)}, u32[]{:S(2)}) async-start(bf16[16,16,128,32]{2,3,1,0:T(8,128)(2,1)} %constant_dynamic-update-slice_fusion), calls=%async_computation | async-start | bytes 4194304 | tf_op jit(solution)/shard_map/all_to_all | solution.py:98
  731.8 207.5 %all-gather.2.cloned.1.call-start = ((), (), s32[]{:S(2)}) async-start(), calls=%async_computation.1 | async-start | bytes 18874368 | tf_op jit(solution)/shard_map/all_gather | solution.py:108
Sparse Core Ops, SparseCore 0:
  766.7 172.6 all-gather.1
